TPU v7x, 32 devices: a whole 2x2x4 slice. The times are simulated.
32 devices in a mesh: groups: 2 (over y), wide: 4 (over z), tp: 2 (over x), sub: 2 (over core).
Axes of the slice: x: 2, y: 2, z: 4, core: 2. Of those that a mesh axis runs over, the one named last changes fastest.
Arguments:
- hidden: bfloat16 [2, 4096, 8192], P(None, ('groups', 'wide'), ('tp', 'sub')), parts along dimension 1, may hold values from -40 to 40
- target_subgroup: int32 [4096, 1], P(('groups', 'wide')), parts along dimension 0, may hold values from 0 to 3; in each aligned block of 512 rows (0 to 511, 512 to 1023, ...) at most 256 rows name the same one
- token_position: int32 [4096], P(('groups', 'wide')), parts along dimension 0, may hold values from 0 to 4095
- adapter_of_row: int32 [4096], P(('groups', 'wide')), parts along dimension 0, may hold values from 0 to 7
- request_length: int32 [4096], P(('groups', 'wide')), parts along dimension 0, may hold values from 1 to 4096
- input_norm_scale: bfloat16 [2, 8192], P(None, ('tp', 'sub')), may hold values from 0.099609375 to 1.8984375
- key_value_weight: bfloat16 [2, 8192, 2048], P(None, ('tp', 'sub')), may hold values from -0.0625 to 0.0625
- adapter_down_weight: bfloat16 [2, 8192, 128], P(None, ('tp', 'sub')), may hold values from -0.0625 to 0.0625
- adapter_up_weight: bfloat16 [2, 128, 2048], P(None, None, ('tp', 'sub')), may hold values from -0.75 to 0.75
Outputs:
- kv_cache: bfloat16 [2, 8192, 2048], P(None, ('groups', 'wide'), ('tp', 'sub')), parts along dimension 1
There are 2 independent parts, one for each index of `groups`. A program takes and returns all parts, laid end to end along the dimension named above; an argument that names none is the same for every part. Nothing has to cross between parts.
Inputs may be any that keep to these rules, and one draw needn't show every extreme that they name: `target_subgroup`: in the rows of one holder no serving subgroup is named by more than 256 rows, a bound that some block reaches.
All inputs are finite; a program needn't handle non-finite values.
Results may differ from a plain program's by a relative error of at most 0.0054.
Values may be sent and summed in bfloat16 or wider, within the bound.
A program may use at most 192 MiB of HBM per device.

v0:
```python
import jax
import jax.numpy as jnp
from jax import lax
from jax.sharding import PartitionSpec as P

MODEL_WIDTH = 8192
HEAD_SIZE = 128
ADAPTER_COUNT = 8
ADAPTER_RANK = 16


EPS = 1e-05
ROPE_BASE = 500000.0
ADAPTER_SCALE = 2.0


def rotate(fresh, position):
    count = fresh.shape[0]
    heads = fresh.shape[1] // (2 * HEAD_SIZE)
    blocks = fresh.reshape(count, heads, 2, HEAD_SIZE)
    half = HEAD_SIZE // 2
    freq = ROPE_BASE ** (-(jnp.arange(half, dtype=jnp.float32) * 2.0 / HEAD_SIZE))
    angle = position.astype(jnp.float32)[:, None] * freq[None, :]
    cosine = jnp.cos(angle)[:, None, :]
    sine = jnp.sin(angle)[:, None, :]
    keys = blocks[:, :, 0]
    first = keys[..., :half]
    second = keys[..., half:]
    turned = jnp.concatenate([first * cosine - second * sine, second * cosine + first * sine], -1)
    return jnp.stack([turned, blocks[:, :, 1]], 2).reshape(count, heads * 2 * HEAD_SIZE)


def rebuild_layer_cache(rows_h, gain, weight, down_map, up_map, position, adapter, valid_mask):
    wide_rows = rows_h.astype(jnp.float32)
    partial_ss = jnp.sum(wide_rows * wide_rows, 1)
    scaled = (wide_rows * gain.astype(jnp.float32)[None, :]).astype(jnp.bfloat16)
    partial_down = jnp.dot(scaled, down_map, preferred_element_type=jnp.float32)
    total_ss, down_projected = lax.psum((partial_ss, partial_down), ("tp", "sub"))
    adapter_scaling = lax.rsqrt(total_ss / MODEL_WIDTH + EPS)
    partial_base = jnp.dot(scaled, weight, preferred_element_type=jnp.float32)
    base = lax.psum_scatter(partial_base, ("tp", "sub"), scatter_dimension=1, tiled=True)
    owner = jnp.arange(ADAPTER_COUNT * ADAPTER_RANK, dtype=jnp.int32) // ADAPTER_RANK
    picked_adapter = adapter[:, None] == owner[None, :]
    low_rank_rows = jnp.where(
        picked_adapter, ADAPTER_SCALE * adapter_scaling[:, None] * down_projected, 0.0
    ).astype(jnp.bfloat16)
    fresh = adapter_scaling[:, None] * base + jnp.dot(
        low_rank_rows, up_map, preferred_element_type=jnp.float32
    )
    rotated = rotate(fresh, position)
    return jnp.where(valid_mask[:, None], rotated, 0.0).astype(jnp.bfloat16)


def shards(
    hidden,
    target_subgroup,
    token_position,
    adapter_of_row,
    request_length,
    input_norm_scale,
    key_value_weight,
    adapter_down_weight,
    adapter_up_weight,
):
    width = lax.axis_size("wide")
    layer_list = hidden.shape[0]
    slots = hidden.shape[1]
    capacity = 2 * slots // width
    target = target_subgroup[:, 0]
    onehot = (target[:, None] == jnp.arange(width, dtype=jnp.int32)[None, :]).astype(jnp.int32)
    rank = jnp.sum(jnp.cumsum(onehot, 0) * onehot, 1) - 1
    place = target * capacity + rank
    source = (
        jnp.zeros((width * capacity,), jnp.int32).at[place].set(jnp.arange(slots, dtype=jnp.int32))
    )
    filled = jnp.zeros((width * capacity,), jnp.int32).at[place].set(1)
    valid_own = token_position < request_length
    taken = jnp.take(hidden, source, axis=1)
    outgoing = jnp.where(filled[None, :, None] > 0, taken, jnp.zeros_like(taken))
    meta = jnp.stack(
        [
            jnp.take(token_position, source),
            jnp.take(adapter_of_row, source),
            jnp.take(valid_own.astype(jnp.int32), source) * filled,
        ],
        1,
    )[None]
    arrived = lax.all_to_all(outgoing, "wide", split_axis=1, concat_axis=1, tiled=True)
    info = lax.all_to_all(meta, "wide", split_axis=1, concat_axis=1, tiled=True)[0]
    position = info[:, 0]
    adapter = info[:, 1]
    valid_mask = info[:, 2] > 0
    results = [
        rebuild_layer_cache(
            arrived[layer_number],
            input_norm_scale[layer_number],
            key_value_weight[layer_number],
            adapter_down_weight[layer_number],
            adapter_up_weight[layer_number],
            position,
            adapter,
            valid_mask,
        )
        for layer_number in range(layer_list)
    ]
    return jnp.stack(results)


def solution(mesh):
    return jax.shard_map(
        shards,
        mesh=mesh,
        in_specs=(
            P(None, ("groups", "wide"), ("tp", "sub")),
            P(("groups", "wide"), None),
            P(("groups", "wide")),
            P(("groups", "wide")),
            P(("groups", "wide")),
            P(None, ("tp", "sub")),
            P(None, ("tp", "sub"), None),
            P(None, ("tp", "sub"), None),
            P(None, None, ("tp", "sub")),
        ),
        out_specs=P(None, ("groups", "wide"), ("tp", "sub")),
        check_vma=False,
    )
```

profile of v0, /device:TPU:0, one launch (start us, length us, event | category | flops | bytes accessed | tf_op | source)
XLA Modules:
  0.0 537.8 jit_solution(1451770309239018447)
XLA Ops:
  12.8 6.2 %gather_fusion.1 = s32[1024]{0:T(1024)S(1)} fusion(s32[512]{0:T(512)} %param.13, s32[1024]{0:T(1024)S(1)} %fusion.43), kind=kCustom, calls=%fused_computation.clone | custom fusion | bytes 12288 | tf_op jit(solution)/shard_map/jit(_take)/gather | solution.py:82
  19.0 49.3 %gather_fusion = bf16[1024,2,2048]{2,0,1:T(8,128)(2,1)} fusion(bf16[2,512,2048]{2,1,0:T(8,128)(2,1)} %param.11, s32[1024]{0:T(1024)S(1)} %fusion.43), kind=kCustom, calls=%fused_computation.3 | custom fusion | bytes 16781312 | tf_op jit(solution)/shard_map/jit(_take)/gather | solution.py:78
  70.7 4.9 select_bitcast_fusion
  75.6 24.9 %copy.31 = bf16[2,1024,2048]{2,0,1:T(2,128)(2,1)} copy(bf16[2,1024,2048]{2,1,0:T(8,128)(2,1)S(1)} %select_bitcast_fusion) | data formatting | bytes 16777216 | tf_op jit(solution)/shard_map/jit(_where)/select_n | solution.py:79
  100.5 6.6 %all-to-all-start.1 = ((bf16[2,1024,2048]{2,0,1:T(2,128)(2,1)}), bf16[2,1024,2048]{2,0,1:T(2,128)(2,1)}, u32[]{:S(2)}, u32[]{:S(2)}) async-start(bf16[2,1024,2048]{2,0,1:T(2,128)(2,1)} %copy.31), calls=%async_computation.1 | async-start | bytes 16777216 | tf_op jit(solution)/shard_map/all_to_all | solution.py:88
  107.3 183.7 %all-to-all-done.1 = bf16[2,1024,2048]{2,0,1:T(2,128)(2,1)} async-done(((bf16[2,1024,2048]{2,0,1:T(2,128)(2,1)}), bf16[2,1024,2048]{2,0,1:T(2,128)(2,1)}, u32[]{:S(2)}, u32[]{:S(2)}) %all-to-all-start.1) | async-done | bytes 8388640 | tf_op jit(solution)/shard_map/all_to_all | solution.py:88
  291.1 16.5 %fusion.54 = (bf16[1,1024,2048]{2,0,1:T(2,128)(2,1)S(1)}, bf16[1,1024,2048]{2,0,1:T(2,128)(2,1)S(1)}) fusion(bf16[2,1024,2048]{2,0,1:T(2,128)(2,1)} %all-to-all-done.1), kind=kLoop, calls=%fused_computation.105 | loop fusion | bytes 16777216 | tf_op jit(solution)/shard_map/slice | solution.py:95
  307.6 3.2 copy-done.2
  310.8 3.2 fusion.12
  314.0 3.2 fusion.15
  317.3 16.7 %fusion.6 = f32[1024,2048]{1,0:T(8,128)} fusion(bf16[2,2048,2048]{2,1,0:T(8,128)(2,1)} %param.17, f32[2048]{0:T(1024)S(1)} %bitcast.85, bf16[1,1024,2048]{2,0,1:T(2,128)(2,1)} %copy-done.2), kind=kOutput, calls=%fused_computation.16 | convolution fusion | flops 8596226048 | bytes 25174016 | tf_op jit(solution)/shard_map/dot_general | solution.py:40
  334.3 16.7 %fusion.4 = f32[1024,2048]{1,0:T(8,128)} fusion(bf16[2,2048,2048]{2,1,0:T(8,128)(2,1)} %param.17, f32[2048]{0:T(1024)S(1)} %bitcast.83, bf16[1,1024,2048]{2,0,1:T(2,128)(2,1)} %copy-done.3), kind=kOutput, calls=%fused_computation.14 | convolution fusion | flops 8596226048 | bytes 25174016 | tf_op jit(solution)/shard_map/dot_general | solution.py:40
  351.7 6.8 %gather_fusion.3 = s32[1024]{0:T(1024)S(1)} fusion(s32[512]{0:T(512)S(1)} %compare_convert_fusion, s32[1024]{0:T(1024)S(1)} %fusion.43), kind=kCustom, calls=%fused_computation.2.clone | custom fusion | bytes 12288 | tf_op jit(solution)/shard_map/jit(_take)/gather | solution.py:84
  358.6 6.9 %gather_fusion.2 = s32[1024]{0:T(1024)S(1)} fusion(s32[512]{0:T(512)S(1)} %copy-done, s32[1024]{0:T(1024)S(1)} %fusion.43), kind=kCustom, calls=%fused_computation.1.clone | custom fusion | bytes 12288 | tf_op jit(solution)/shard_map/jit(_take)/gather | solution.py:83
  369.3 3.7 all-to-all-start
  373.0 5.5 %all-to-all-done = s32[4,1,768]{2,1,0:T(1,128)S(1)} async-done(((s32[4,1,768]{2,1,0:T(1,128)}), s32[4,1,768]{2,1,0:T(1,128)S(1)}, u32[]{:S(2)}, u32[]{:S(2)}) %all-to-all-start) | async-done | bytes 12320 | tf_op jit(solution)/shard_map/all_to_all | solution.py:89
  382.7 12.3 %fusion = (f32[1024]{0:T(1024)S(1)}, f32[1024]{0:T(1024)S(1)}) fusion(bf16[1,1024,2048]{2,0,1:T(2,128)(2,1)} %copy-done.2, bf16[1,1024,2048]{2,0,1:T(2,128)(2,1)} %copy-done.3), kind=kLoop, calls=%fused_computation.10 | loop fusion | flops 12580864 | bytes 8396800 | tf_op jit(solution)/shard_map/reduce_sum | solution.py:35
  395.0 6.6 %all-reduce = (f32[1024]{0:T(1024)S(1)}, f32[1024]{0:T(1024)S(1)}) all-reduce(f32[1024]{0:T(1024)S(1)} %get-tuple-element.33, f32[1024]{0:T(1024)S(1)} %get-tuple-element.32), channel_id=1, replica_groups=mesh['groups'=2,'wide'=4,'tp'=2,'sub'=2] {'tp','sub'}, use_global_device_ids=true, to_apply=%region_10.12 | all-reduce | flops 2048 | bytes 16384 | tf_op jit(solution)/shard_map/psum | solution.py:38
  401.7 26.1 %reduce-scatter.3.cloned.1.call-done = f32[1024,512]{1,0:T(8,128)} async-done(((f32[1024,2048]{1,0:T(8,128)}), f32[1024,512]{1,0:T(8,128)}) %reduce-scatter.3.cloned.1.call-update) | async-done | bytes 2097168 | tf_op jit(solution)/shard_map/reduce_scatter | solution.py:41
  427.8 3.7 multiply_add_fusion.1
  436.2 65.9 %reduce-scatter.5.cloned.1.call-done = f32[1024,512]{1,0:T(8,128)} async-done(((f32[1024,2048]{1,0:T(8,128)}), f32[1024,512]{1,0:T(8,128)}) %reduce-scatter.5.cloned.1.call-update) | async-done | bytes 2097168 | tf_op jit(solution)/shard_map/reduce_scatter | solution.py:41
  502.1 3.7 multiply_add_fusion
  505.9 3.5 reshape.242
  509.4 4.0 fusion.55
  (74 shorter events, 40.3 us)
Async XLA Ops:
  6.5 352.0 %copy-start = (s32[512]{0:T(512)S(1)}, s32[512]{0:T(512)}, u32[]{:S(2)}) copy-start(s32[512]{0:T(512)} %param.14) | copy-start | bytes 6148
  100.5 6.8 %copy-start.7 = (bf16[2,2048]{1,0:T(2,128)(2,1)S(1)}, bf16[2,2048]{1,0:T(2,128)(2,1)}, u32[]{:S(2)}) copy-start(bf16[2,2048]{1,0:T(2,128)(2,1)} %param.16) | copy-start | bytes 24580
  100.5 190.6 %all-to-all-start.1 = ((bf16[2,1024,2048]{2,0,1:T(2,128)(2,1)}), bf16[2,1024,2048]{2,0,1:T(2,128)(2,1)}, u32[]{:S(2)}, u32[]{:S(2)}) async-start(bf16[2,1024,2048]{2,0,1:T(2,128)(2,1)} %copy.31), calls=%async_computation.1 | async-start | bytes 16777216 | tf_op jit(solution)/shard_map/all_to_all | solution.py:88
  107.1 294.6 %all-reduce.4.cloned.1.call-start = ((), (), s32[]{:S(2)}) async-start(), calls=%async_computation.6 | async-start | bytes 2097152 | tf_op jit(solution)/shard_map/psum | solution.py:38
  107.3 203.5 %copy-start.9 = (bf16[2,2048,128]{2,1,0:T(8,128)(2,1)S(1)}, bf16[2,2048,128]{2,1,0:T(8,128)(2,1)}, u32[]{:S(2)}) copy-start(bf16[2,2048,128]{2,1,0:T(8,128)(2,1)} %param.18) | copy-start | bytes 3145732
  307.6 3.2 copy-start.2
  307.6 6.4 %copy-start.3 = (bf16[1,1024,2048]{2,0,1:T(2,128)(2,1)}, bf16[1,1024,2048]{2,0,1:T(2,128)(2,1)S(1)}, u32[]{:S(2)}) copy-start(bf16[1,1024,2048]{2,0,1:T(2,128)(2,1)S(1)} %get-tuple-element.13) | copy-start | bytes 12582916
  317.2 110.6 %reduce-scatter.3.cloned.1.call-start = ((), (), s32[]{:S(2)}) async-start(), calls=%async_computation.4 | async-start | bytes 10485760 | tf_op jit(solution)/shard_map/reduce_scatter | solution.py:41
  334.0 168.1 %reduce-scatter.5.cloned.1.call-start = ((), (), s32[]{:S(2)}) async-start(), calls=%async_computation.5 | async-start | bytes 10485760 | tf_op jit(solution)/shard_map/reduce_scatter | solution.py:41
  351.0 0.7 copy-start.1
  351.0 0.7 copy-start.8
  369.3 9.3 %all-to-all-start = ((s32[4,1,768]{2,1,0:T(1,128)}), s32[4,1,768]{2,1,0:T(1,128)S(1)}, u32[]{:S(2)}, u32[]{:S(2)}) async-start(s32[4,1,768]{2,1,0:T(1,128)} %reshape.312), calls=%async_computation | async-start | bytes 24576 | tf_op jit(solution)/shard_map/all_to_all | solution.py:89
  382.7 45.1 %copy-start.6 = (bf16[2,128,512]{2,1,0:T(8,128)(2,1)S(1)}, bf16[2,128,512]{2,1,0:T(8,128)(2,1)}, u32[]{:S(2)}) copy-start(bf16[2,128,512]{2,1,0:T(8,128)(2,1)} %param.19) | copy-start | bytes 786436
  434.1 79.3 %copy-start.4 = (f32[1024,2,2,128]{3,2,1,0:T(2,128)}, f32[1024,2,2,128]{3,2,1,0:T(2,128)S(1)}, u32[]{:S(2)}) copy-start(f32[1024,2,2,128]{3,2,1,0:T(2,128)S(1)} %reshape.240) | copy-start | bytes 6291460
  513.4 9.4 %slice-start = ((f32[1024,2,2,128]{3,2,1,0:T(2,128)}), f32[1024,2,1,128]{3,2,1,0:T(1,128)S(1)}, s32[]{:S(2)}) async-start(f32[1024,2,2,128]{3,2,1,0:T(2,128)} %copy-done.4), calls=%async_computation.7 | async-start | bytes 2097152 | tf_op jit(solution)/shard_map/slice | solution.py:26
  524.3 4.8 copy-start.5
Sparse Core Ops, SparseCore 0:
  317.4 35.2 all-reduce.3
  355.4 72.3 reduce-scatter.2
  430.4 71.6 reduce-scatter.4
where the time goes:
time: 545 us; the launch traced here: 538 us
  waiting for transfers between devices  281 us (52%)
  local copies, waits for them, and re-layouts  140 us (26%)
  matrix products  47.2 us (9%)
  other arithmetic  38.1 us (7%)
  between operations  13.7 us (3%)
  starting transfers between devices  10.8 us (2%)
  blocking collectives  6.63 us (1%)
    all_to_all x1, waiting for transfers between devices, shards(): lax.all_to_all(outgoing, 'wide', split_axis=1, concat_axis=1, tiled=True)  184 us
    reduce_scatter x2, waiting for transfers between devices, rebuild_layer_cache(): lax.psum_scatter(partial_base, ('tp', 'sub'), scatter_dimension=1, tiled=...  92 us
    gather x1, local copies, waits for them, and re-layouts, shards(): taken = jnp.take(hidden, source, axis=1)  49.3 us
    dot_general x2, matrix products, rebuild_layer_cache(): partial_base = jnp.dot(scaled, weight, preferred_element_type=jnp.float32)  33.4 us
    select_n x1, local copies, waits for them, and re-layouts, shards(): jnp.where(filled[None, :, None] > 0, taken, jnp.zeros_like(taken))  24.9 us
    slice x1, local copies, waits for them, and re-layouts, shards(): arrived[layer_number]  16.5 us
    reduce_sum x1, other arithmetic, rebuild_layer_cache(): partial_ss = jnp.sum(wide_rows * wide_rows, 1)  12.3 us
  transfers between devices with their start and end apart: 5, of which 4 were waited for; matrix products, arithmetic and copies ran while one was open for 14% of the time, Pallas kernels for 0%

commit v1 on v0

v1 whole, which is shorter than its diff:
```python
import functools

import jax
import jax.numpy as jnp
from jax import lax
from jax.experimental import pallas as pl
from jax.experimental.pallas import tpu as pltpu
from jax.sharding import PartitionSpec as P

MODEL_WIDTH = 8192
HEAD_SIZE = 128
ADAPTER_COUNT = 8
ADAPTER_RANK = 16
EPS = 1e-05
ROPE_BASE = 500000.0
ADAPTER_SCALE = 2.0
UNIT = HEAD_SIZE
STAT_ROWS = 24
F32, BF16 = jnp.float32, jnp.bfloat16


def restore_kernel(
    sizes,
    hidden_hbm,
    weight_hbm,
    down_hbm,
    up_ref,
    gain_ref,
    target_ref,
    position_ref,
    adapter_ref,
    length_ref,
    freq_ref,
    out_hbm,
    hidden_buf,
    scaled,
    weight_buf,
    down_buf,
    own_acc,
    core_out,
    core_in,
    x_out,
    x_in,
    stat_out,
    stat_in,
    low_rows,
    scale_rows,
    cos_tab,
    sin_tab,
    pick,
    z_out,
    hidden_sem,
    weight_sem,
    down_sem,
    core_send,
    core_recv,
    x_send,
    x_recv,
    stat_send,
    stat_recv,
    z_send,
    z_recv,
    z_local,
):
    layers, slots, features, block, tp_size, sub_size, width = sizes
    capacity = 2 * slots // width
    units = block // UNIT
    chunks = layers * units
    peers = tp_size * sub_size
    half_cols = tp_size * UNIT

    tp = lax.axis_index("tp")
    sub = lax.axis_index("sub")
    wide = lax.axis_index("wide")

    def peer_id(d):
        dt, ds = d // sub_size, d % sub_size
        return {"tp": lax.rem(tp + dt, tp_size), "sub": lax.rem(sub + ds, sub_size)}

    def wide_id(dw):
        return {"wide": lax.rem(wide + dw, width)}

    def hidden_copy(layer):
        return pltpu.make_async_copy(hidden_hbm.at[layer], hidden_buf.at[layer], hidden_sem.at[layer])

    def down_copy(layer):
        return pltpu.make_async_copy(down_hbm.at[layer], down_buf.at[layer], down_sem.at[layer])

    def weight_copies(chunk):
        layer, unit = chunk // units, chunk % units
        copies = []
        for ds in range(sub_size):
            for dt in range(tp_size):
                t = lax.rem(tp + dt, tp_size)
                s = lax.rem(sub + ds, sub_size)
                column = pl.multiple_of((t * sub_size + s) * block + unit * UNIT, UNIT)
                place = ds * tp_size + dt
                copies.append(
                    pltpu.make_async_copy(
                        weight_hbm.at[layer, :, pl.ds(column, UNIT)],
                        weight_buf.at[chunk, :, pl.ds(place * UNIT, UNIT)],
                        weight_sem.at[chunk, place],
                    )
                )
        return copies

    def core_copy(chunk):
        return pltpu.make_async_remote_copy(
            src_ref=core_out.at[chunk],
            dst_ref=core_in.at[chunk],
            send_sem=core_send.at[chunk],
            recv_sem=core_recv.at[chunk],
            device_id={"sub": lax.rem(sub + 1, sub_size)},
            device_id_type=pl.DeviceIdType.MESH,
        )

    def x_copy(chunk, dt):
        return pltpu.make_async_remote_copy(
            src_ref=x_out.at[chunk, dt - 1],
            dst_ref=x_in.at[chunk, dt - 1],
            send_sem=x_send.at[chunk, dt - 1],
            recv_sem=x_recv.at[chunk, dt - 1],
            device_id={"tp": lax.rem(tp + dt, tp_size)},
            device_id_type=pl.DeviceIdType.MESH,
        )

    def stat_copy(layer, d):
        return pltpu.make_async_remote_copy(
            src_ref=stat_out.at[layer],
            dst_ref=stat_in.at[layer, d - 1],
            send_sem=stat_send.at[layer, d - 1],
            recv_sem=stat_recv.at[layer, d - 1],
            device_id=peer_id(d),
            device_id_type=pl.DeviceIdType.MESH,
        )

    def z_copy(chunk, dw, holder):
        layer, unit = chunk // units, chunk % units
        goal = lax.rem(wide + dw, width)
        return pltpu.make_async_remote_copy(
            src_ref=z_out.at[chunk, pl.ds(pl.multiple_of(goal * capacity, 16), capacity), :],
            dst_ref=out_hbm.at[
                layer,
                pl.ds(pl.multiple_of(holder * capacity, 16), capacity),
                pl.ds(pl.multiple_of(unit * UNIT, UNIT), UNIT),
            ],
            send_sem=z_send.at[chunk, dw - 1],
            recv_sem=z_recv.at[chunk, dw - 1],
            device_id=wide_id(dw),
            device_id_type=pl.DeviceIdType.MESH,
        )

    def z_own(chunk):
        layer, unit = chunk // units, chunk % units
        rows = pl.ds(pl.multiple_of(wide * capacity, 16), capacity)
        return pltpu.make_async_copy(
            z_out.at[chunk, rows, :],
            out_hbm.at[layer, rows, pl.ds(pl.multiple_of(unit * UNIT, UNIT), UNIT)],
            z_local.at[chunk],
        )

    def scale_hidden(layer):
        hidden_copy(layer).wait()
        step_rows = 128

        @pl.loop(0, slots // step_rows)
        def _(r):
            rows = pl.ds(pl.multiple_of(r * step_rows, step_rows), step_rows)
            squares = jnp.zeros((step_rows, 128), F32)
            for k in range(features // 128):
                columns = pl.ds(k * 128, 128)
                values = hidden_buf[layer, rows, columns].astype(F32)
                gain = gain_ref[layer, columns].astype(F32)
                squares += values * values
                scaled[layer, rows, columns] = (values * gain[None, :]).astype(BF16)
            total = jnp.sum(squares.T, axis=0, keepdims=True)
            stat_out[layer, pl.ds(ADAPTER_RANK, 8), rows] = jnp.broadcast_to(total, (8, step_rows))

    def send_stats(layer):
        down_copy(layer).wait()
        down = jnp.dot(scaled[layer], down_buf[layer], preferred_element_type=F32).T
        adapter = adapter_ref[...]
        picked = jnp.zeros((ADAPTER_RANK, slots), F32)
        for a in range(ADAPTER_COUNT):
            picked += jnp.where(adapter == a, down[a * ADAPTER_RANK : (a + 1) * ADAPTER_RANK], 0.0)
        stat_out[layer, pl.ds(0, ADAPTER_RANK), :] = picked
        for d in range(1, peers):
            stat_copy(layer, d).start()

    def take_stats(layer):
        total = stat_out[layer]
        for d in range(1, peers):
            stat_copy(layer, d).wait_recv()
            total += stat_in[layer, d - 1]
        scale = lax.rsqrt(total[ADAPTER_RANK : ADAPTER_RANK + 1] / MODEL_WIDTH + EPS)
        low = ADAPTER_SCALE * scale * total[:ADAPTER_RANK]
        adapter = adapter_ref[...]
        spread = jnp.concatenate(
            [jnp.where(adapter == a, low, 0.0) for a in range(ADAPTER_COUNT)], axis=0
        )
        low_rows[layer] = spread.T.astype(BF16)
        scale_rows[layer] = jnp.broadcast_to(scale, (UNIT, slots)).T

    def make_tables():
        position = position_ref[...]
        angle = freq_ref[...] * position.astype(F32)
        cosine, sine = jnp.cos(angle), jnp.sin(angle)
        cos_tab[0] = jnp.concatenate([cosine, cosine], axis=0).T
        sin_tab[0] = jnp.concatenate([-sine, sine], axis=0).T
        cos_tab[1] = jnp.ones((slots, UNIT), F32)
        sin_tab[1] = jnp.zeros((slots, UNIT), F32)
        target = target_ref[...]
        lanes = max(width, 16)
        onehot = lax.broadcasted_iota(jnp.int32, (lanes, slots), 0) == target
        before = lax.broadcasted_iota(jnp.int32, (slots, slots), 0) <= lax.broadcasted_iota(
            jnp.int32, (slots, slots), 1
        )
        counted = jnp.dot(
            jnp.where(onehot, 1.0, 0.0).astype(BF16),
            jnp.where(before, 1.0, 0.0).astype(BF16),
            preferred_element_type=F32,
        )
        rank = jnp.sum(jnp.where(onehot, counted, 0.0), axis=0, keepdims=True).astype(jnp.int32) - 1
        place = target * capacity + rank
        place = jnp.where(position < length_ref[...], place, -1)

        @pl.loop(0, width * capacity // 128)
        def _(r):
            index = lax.broadcasted_iota(jnp.int32, (128, slots), 0) + r * 128
            pick[pl.ds(pl.multiple_of(r * 128, 128), 128), :] = jnp.where(
                index == place, 1.0, 0.0
            ).astype(BF16)

    def project(chunk):
        for copy in weight_copies(chunk):
            copy.wait()
        layer = chunk // units
        core_out[chunk] = jnp.dot(
            scaled[layer], weight_buf[chunk, :, half_cols:], preferred_element_type=F32
        ).astype(BF16)
        core_copy(chunk).start()
        own_acc[chunk] = jnp.dot(
            scaled[layer], weight_buf[chunk, :, :half_cols], preferred_element_type=F32
        )

    def pass_on(chunk):
        core_copy(chunk).wait_recv()
        for dt in range(1, tp_size):
            columns = pl.ds(dt * UNIT, UNIT)
            x_out[chunk, dt - 1] = (
                own_acc[chunk, :, columns] + core_in[chunk, :, columns].astype(F32)
            ).astype(BF16)
            x_copy(chunk, dt).start()

    def finish(chunk):
        layer, unit = chunk // units, chunk % units
        base = own_acc[chunk, :, pl.ds(0, UNIT)] + core_in[chunk, :, pl.ds(0, UNIT)].astype(F32)
        for dt in range(1, tp_size):
            x_copy(chunk, dt).wait_recv()
            base += x_in[chunk, dt - 1].astype(F32)
        fresh = scale_rows[layer] * base + jnp.dot(
            low_rows[layer], up_ref[layer, unit], preferred_element_type=F32
        )
        kind = unit % 2
        rotated = (
            fresh * cos_tab[kind] + pltpu.roll(fresh, HEAD_SIZE // 2, 1) * sin_tab[kind]
        ).astype(BF16)
        z_out[chunk] = jnp.dot(pick[...], rotated, preferred_element_type=F32).astype(BF16)
        for dw in range(width - 1, 0, -1):
            z_copy(chunk, dw, wide).start()
        z_own(chunk).start()

    hidden_copy(0).start()
    for copy in weight_copies(0):
        copy.start()
    down_copy(0).start()

    barrier = pltpu.get_barrier_semaphore()
    for d in range(1, peers):
        pl.semaphore_signal(barrier, inc=1, device_id=peer_id(d), device_id_type=pl.DeviceIdType.MESH)
    for dw in range(1, width):
        pl.semaphore_signal(barrier, inc=1, device_id=wide_id(dw), device_id_type=pl.DeviceIdType.MESH)

    @pl.loop(1, chunks)
    def _(chunk):
        for copy in weight_copies(chunk):
            copy.start()

    for layer in range(1, layers):
        hidden_copy(layer).start()
        down_copy(layer).start()
    scale_hidden(0)
    pl.semaphore_wait(barrier, peers - 1 + width - 1)

    @pl.loop(0, chunks + 2)
    def _(step):
        @pl.when(step < chunks)
        def _():
            project(step)

        @pl.when(step == 0)
        def _():
            send_stats(0)
            pass_on(0)
            make_tables()

        @pl.when(step == 1)
        def _():
            take_stats(0)
            for layer in range(1, layers):
                scale_hidden(layer)
                send_stats(layer)

        @pl.when((step >= 2) & (step <= chunks))
        def _():
            pass_on(step - 1)

        @pl.when(step >= 2)
        def _():
            finish(step - 2)

        @pl.when(step == 2)
        def _():
            for layer in range(1, layers):
                take_stats(layer)

    for layer in range(layers):
        for d in range(1, peers):
            stat_copy(layer, d).wait_send()

    @pl.loop(0, chunks)
    def _(chunk):
        core_copy(chunk).wait_send()
        for dt in range(1, tp_size):
            x_copy(chunk, dt).wait_send()
        for dw in range(1, width):
            z_copy(chunk, dw, wide).wait_send()
            z_copy(chunk, dw, lax.rem(wide - dw + width, width)).wait_recv()
        z_own(chunk).wait()


def shards(
    sizes_of_mesh,
    hidden,
    target_subgroup,
    token_position,
    adapter_of_row,
    request_length,
    input_norm_scale,
    key_value_weight,
    adapter_down_weight,
    adapter_up_weight,
):
    tp_size, sub_size, width = sizes_of_mesh
    layers, slots, features = hidden.shape
    block = adapter_up_weight.shape[2]
    units = block // UNIT
    chunks = layers * units
    peers = tp_size * sub_size
    capacity = 2 * slots // width
    half = HEAD_SIZE // 2
    freq = ROPE_BASE ** (-(jnp.arange(half, dtype=F32) * 2.0 / HEAD_SIZE))
    up_units = adapter_up_weight.reshape(layers, -1, units, UNIT).transpose(0, 2, 1, 3)
    sizes = (layers, slots, features, block, tp_size, sub_size, width)
    hbm = pl.BlockSpec(memory_space=pl.ANY)
    vmem = pl.BlockSpec(memory_space=pltpu.VMEM)
    dma = pltpu.SemaphoreType.DMA
    columns = key_value_weight.shape[2]
    ranks = adapter_down_weight.shape[2]
    return pl.pallas_call(
        functools.partial(restore_kernel, sizes),
        out_shape=jax.ShapeDtypeStruct((layers, width * capacity, block), BF16),
        in_specs=[hbm, hbm, hbm] + [vmem] * 7,
        out_specs=hbm,
        scratch_shapes=[
            pltpu.VMEM((layers, slots, features), BF16),
            pltpu.VMEM((layers, slots, features), BF16),
            pltpu.VMEM((chunks, features, peers * UNIT), BF16),
            pltpu.VMEM((layers, features, ranks), BF16),
            pltpu.VMEM((chunks, slots, tp_size * UNIT), F32),
            pltpu.VMEM((chunks, slots, tp_size * UNIT), BF16),
            pltpu.VMEM((chunks, slots, tp_size * UNIT), BF16),
            pltpu.VMEM((chunks, tp_size - 1, slots, UNIT), BF16),
            pltpu.VMEM((chunks, tp_size - 1, slots, UNIT), BF16),
            pltpu.VMEM((layers, STAT_ROWS, slots), F32),
            pltpu.VMEM((layers, peers - 1, STAT_ROWS, slots), F32),
            pltpu.VMEM((layers, slots, ranks), BF16),
            pltpu.VMEM((layers, slots, UNIT), F32),
            pltpu.VMEM((2, slots, UNIT), F32),
            pltpu.VMEM((2, slots, UNIT), F32),
            pltpu.VMEM((width * capacity, slots), BF16),
            pltpu.VMEM((chunks, width * capacity, UNIT), BF16),
            dma((layers,)),
            dma((chunks, peers)),
            dma((layers,)),
            dma((chunks,)),
            dma((chunks,)),
            dma((chunks, tp_size - 1)),
            dma((chunks, tp_size - 1)),
            dma((layers, peers - 1)),
            dma((layers, peers - 1)),
            dma((chunks, width - 1)),
            dma((chunks, width - 1)),
            dma((chunks,)),
        ],
        compiler_params=pltpu.CompilerParams(
            collective_id=0, has_side_effects=True, vmem_limit_bytes=56 * 1024 * 1024
        ),
        cost_estimate=pl.CostEstimate(
            flops=2 * layers * slots * features * columns,
            bytes_accessed=2 * layers * features * columns,
            transcendentals=0,
        ),
        name="restore_rows",
    )(
        hidden,
        key_value_weight,
        adapter_down_weight,
        up_units,
        input_norm_scale,
        target_subgroup.reshape(1, slots),
        token_position.reshape(1, slots),
        adapter_of_row.reshape(1, slots),
        request_length.reshape(1, slots),
        freq.reshape(half, 1),
    )


def solution(mesh):
    sizes_of_mesh = (mesh.shape["tp"], mesh.shape["sub"], mesh.shape["wide"])
    return jax.shard_map(
        functools.partial(shards, sizes_of_mesh),
        mesh=mesh,
        in_specs=(
            P(None, ("groups", "wide"), ("tp", "sub")),
            P(("groups", "wide"), None),
            P(("groups", "wide")),
            P(("groups", "wide")),
            P(("groups", "wide")),
            P(None, ("tp", "sub")),
            P(None, ("tp", "sub"), None),
            P(None, ("tp", "sub"), None),
            P(None, None, ("tp", "sub")),
        ),
        out_specs=P(None, ("groups", "wide"), ("tp", "sub")),
        check_vma=False,
    )
```

time: 545 us -> 74.3 us (0.14); the launches traced: 538 us -> 74.1 us
  waiting for transfers between devices: 281 us -> 0 us
  local copies, waits for them, and re-layouts: 140 us -> 5.02 us
  Pallas kernels: 0 us -> 68.4 us
  matrix products: 47.2 us -> 0 us
  other arithmetic: 38.1 us -> 0.62 us
  between operations: 13.7 us -> 0.02 us
  starting transfers between devices: 10.8 us -> 0 us
  blocking collectives: 6.63 us -> 0 us
    all_to_all x2 -> x0, waiting for transfers between devices: 189 us -> none  [the longest x1 184 us: shards(): lax.all_to_all(outgoing, 'wide', split_axis=1, concat_axis=1, tiled=True)]
    reduce_scatter x2 -> x0, waiting for transfers between devices: 92 us -> none  [rebuild_layer_cache(): lax.psum_scatter(partial_base, ('tp', 'sub'), scatter_dimension=1, tiled=...]
    gather x4 -> x0, local copies, waits for them, and re-layouts: 69.2 us -> none  [the longest x1 49.3 us: shards(): taken = jnp.take(hidden, source, axis=1)]
    pallas_call x0 -> x1, Pallas kernels: none -> 68.4 us  [shards(): pl.pallas_call(functools.partial(restore_kernel, sizes), out_shape=jax.Sh...]
    dot_general x6 -> x0, matrix products: 47.2 us -> none  [the longest x2 33.4 us: rebuild_layer_cache(): partial_base = jnp.dot(scaled, weight, preferred_element_type=jnp.float32)]
    select_n x1 -> x0, local copies, waits for them, and re-layouts: 24.9 us -> none  [shards(): jnp.where(filled[None, :, None] > 0, taken, jnp.zeros_like(taken))]
    slice x7 -> x0, local copies, waits for them, and re-layouts: 23.2 us -> none  [the longest x1 16.5 us: shards(): arrived[layer_number]]
    reduce_sum x2 -> x0, other arithmetic: 13 us -> none  [the longest x1 12.3 us: rebuild_layer_cache(): partial_ss = jnp.sum(wide_rows * wide_rows, 1)]
  transfers between devices with their start and end apart: 5 -> 0, of which waited for: 4 -> 0; matrix products, arithmetic and copies ran while one was open for 14% -> 0% of each run, Pallas kernels for 0% -> 0%
where the time goes in v1:
time: 74.3 us; the launch traced here: 74.1 us
  Pallas kernels  68.4 us (92%)
  local copies, waits for them, and re-layouts  5.02 us (7%)
    pallas_call x1, Pallas kernels, shards(): pl.pallas_call(functools.partial(restore_kernel, sizes), out_shape=jax.Sh...  68.4 us
    unnamed x2, local copies, waits for them, and re-layouts  4.16 us

profile of v1, /device:TPU:0, one launch (start us, length us, event | category | flops | bytes accessed | tf_op | source)
XLA Modules:
  0.0 74.1 jit_solution(5188895529305253340)
XLA Ops:
  0.0 0.6 negate_power_fusion.freq_ref
  0.6 1.1 %copy.12 = bf16[2,128,512]{1,2,0:T(8,128)(2,1)S(1)} copy(bf16[2,128,512]{2,1,0:T(8,128)(2,1)} %param.17) | data formatting | bytes 524288 | tf_op args[8]
  1.7 0.9 %copy.13 = bf16[2,128,4,128]{3,1,2,0:T(8,128)(2,1)} copy(bf16[2,128,4,128]{1,3,2,0:T(8,128)(2,1)S(1)} %bitcast.6) | data formatting | bytes 524288 | tf_op jit(solution)/shard_map/reshape | solution.py:363
  2.6 68.4 %restore_rows.1 = bf16[2,1024,512]{2,1,0:T(8,128)(2,1)} custom-call(bf16[2,512,2048]{2,1,0:T(8,128)(2,1)} %hidden_hbm.1, bf16[2,2048,2048]{2,1,0:T(8,128)(2,1)} %weight_hbm.1, bf16[2,2048,128]{2,1,0:T(8,128)(2,1)} %down_hbm.1, bf16[2,4,128,128]{3,2,1,0:T(8,128)(2,1)} %bitcast.7, bf16[2,2048]{1,0:T(2,128)(2,1)} %gain_ref.1, s32[1,512]{1,0:T(1,128)} %bitcast.8, ...), custom_call_target="tpu_custom_call" | custom-call | flops 8589934592 | bytes 16777216 | tf_op jit(solution)/shard_map/restore_rows/pallas_call | solution.py:370
  71.0 3.0 %copy.16 = bf16[2,1024,512]{2,1,0:T(8,128)(2,1)} copy(bf16[2,1024,512]{2,1,0:T(8,128)(2,1)} %restore_rows.1) | data formatting | bytes 4194304

commit v2 on v1

--- a/solution.py
+++ b/solution.py
@@ -2,6 +2,7 @@
 
 import jax
 import jax.numpy as jnp
+import numpy as np
 from jax import lax
 from jax.experimental import pallas as pl
 from jax.experimental.pallas import tpu as pltpu
@@ -259,7 +260,9 @@
             x_copy(chunk, dt).wait_recv()
             base += x_in[chunk, dt - 1].astype(F32)
         fresh = scale_rows[layer] * base + jnp.dot(
-            low_rows[layer], up_ref[layer, unit], preferred_element_type=F32
+            low_rows[layer],
+            up_ref[layer, :, pl.ds(pl.multiple_of(unit * UNIT, UNIT), UNIT)],
+            preferred_element_type=F32,
         )
         kind = unit % 2
         rotated = (
@@ -281,6 +284,8 @@
     for dw in range(1, width):
         pl.semaphore_signal(barrier, inc=1, device_id=wide_id(dw), device_id_type=pl.DeviceIdType.MESH)
 
+    scale_hidden(0)
+
     @pl.loop(1, chunks)
     def _(chunk):
         for copy in weight_copies(chunk):
@@ -289,40 +294,45 @@
     for layer in range(1, layers):
         hidden_copy(layer).start()
         down_copy(layer).start()
-    scale_hidden(0)
     pl.semaphore_wait(barrier, peers - 1 + width - 1)
 
-    @pl.loop(0, chunks + 2)
+    @pl.loop(0, chunks + 1)
     def _(step):
-        @pl.when(step < chunks)
-        def _():
-            project(step)
-
-        @pl.when(step == 0)
-        def _():
-            send_stats(0)
-            pass_on(0)
-            make_tables()
-
-        @pl.when(step == 1)
-        def _():
-            take_stats(0)
+        @pl.when(step == 2)
+        def _():
             for layer in range(1, layers):
                 scale_hidden(layer)
+
+        @pl.when(step < chunks)
+        def _():
+            project(step)
+
+        @pl.when(step == 0)
+        def _():
+            send_stats(0)
+
+        @pl.when(step == 1)
+        def _():
+            make_tables()
+            take_stats(0)
+
+        @pl.when(step == 2)
+        def _():
+            for layer in range(1, layers):
                 send_stats(layer)
 
-        @pl.when((step >= 2) & (step <= chunks))
-        def _():
-            pass_on(step - 1)
-
-        @pl.when(step >= 2)
-        def _():
-            finish(step - 2)
-
-        @pl.when(step == 2)
+        @pl.when(step < chunks)
+        def _():
+            pass_on(step)
+
+        @pl.when(step == 3)
         def _():
             for layer in range(1, layers):
                 take_stats(layer)
+
+        @pl.when(step >= 1)
+        def _():
+            finish(step - 1)
 
     for layer in range(layers):
         for d in range(1, peers):
@@ -359,8 +369,7 @@
     peers = tp_size * sub_size
     capacity = 2 * slots // width
     half = HEAD_SIZE // 2
-    freq = ROPE_BASE ** (-(jnp.arange(half, dtype=F32) * 2.0 / HEAD_SIZE))
-    up_units = adapter_up_weight.reshape(layers, -1, units, UNIT).transpose(0, 2, 1, 3)
+    freq = (ROPE_BASE ** (-np.arange(half) * 2.0 / HEAD_SIZE)).astype(np.float32)
     sizes = (layers, slots, features, block, tp_size, sub_size, width)
     hbm = pl.BlockSpec(memory_space=pl.ANY)
     vmem = pl.BlockSpec(memory_space=pltpu.VMEM)
@@ -416,13 +425,13 @@
         hidden,
         key_value_weight,
         adapter_down_weight,
-        up_units,
+        adapter_up_weight,
         input_norm_scale,
         target_subgroup.reshape(1, slots),
         token_position.reshape(1, slots),
         adapter_of_row.reshape(1, slots),
         request_length.reshape(1, slots),
-        freq.reshape(half, 1),
+        jnp.asarray(freq.reshape(half, 1)),
     )
 
 

time: 74.3 us -> 69.3 us (0.933)
  Pallas kernels: 68.4 us -> 66.1 us
  local copies, waits for them, and re-layouts: 5.02 us -> 3.05 us
    pallas_call x1, Pallas kernels: 68.4 us -> 66.1 us  [shards(): pl.pallas_call(functools.partial(restore_kernel, sizes), out_shape=jax.Sh...]
    unnamed x2 -> x1, local copies, waits for them, and re-layouts: 4.16 us -> 3.05 us
    reshape x1 -> x0, local copies, waits for them, and re-layouts: 0.85 us -> none  [shards(): adapter_up_weight.reshape(layers, -1, units, UNIT).transpose(0, 2, 1, 3)]
where the time goes in v2:
time: 69.3 us; the launch traced here: 69.1 us
  Pallas kernels  66.1 us (95%)
  local copies, waits for them, and re-layouts  3.05 us (4%)
    pallas_call x1, Pallas kernels, shards(): pl.pallas_call(functools.partial(restore_kernel, sizes), out_shape=jax.Sh...  66.1 us
    unnamed x1, local copies, waits for them, and re-layouts  3.05 us

profile of v2, /device:TPU:0, one launch (start us, length us, event | category | flops | bytes accessed | tf_op | source)
XLA Modules:
  0.0 69.1 jit_solution(13049261769966730142)
XLA Ops:
  0.0 66.1 %restore_rows.1 = bf16[2,1024,512]{2,1,0:T(8,128)(2,1)} custom-call(bf16[2,512,2048]{2,1,0:T(8,128)(2,1)} %hidden_hbm.1, bf16[2,2048,2048]{2,1,0:T(8,128)(2,1)} %weight_hbm.1, bf16[2,2048,128]{2,1,0:T(8,128)(2,1)} %down_hbm.1, bf16[2,128,512]{2,1,0:T(8,128)(2,1)} %up_ref.1, bf16[2,2048]{1,0:T(2,128)(2,1)} %gain_ref.1, s32[1,512]{1,0:T(1,128)} %bitcast.4, ...), custom_call_target="tpu_custom_call" | custom-call | flops 8589934592 | bytes 16777216 | tf_op jit(solution)/shard_map/restore_rows/pallas_call | solution.py:379
  66.1 3.0 %copy.12 = bf16[2,1024,512]{2,1,0:T(8,128)(2,1)} copy(bf16[2,1024,512]{2,1,0:T(8,128)(2,1)} %restore_rows.1) | data formatting | bytes 4194304

commit v3 on v2

--- a/solution.py
+++ b/solution.py
@@ -32,7 +32,7 @@
     adapter_ref,
     length_ref,
     freq_ref,
-    out_hbm,
+    held,
     hidden_buf,
     scaled,
     weight_buf,
@@ -136,15 +136,10 @@
         )
 
     def z_copy(chunk, dw, holder):
-        layer, unit = chunk // units, chunk % units
         goal = lax.rem(wide + dw, width)
         return pltpu.make_async_remote_copy(
             src_ref=z_out.at[chunk, pl.ds(pl.multiple_of(goal * capacity, 16), capacity), :],
-            dst_ref=out_hbm.at[
-                layer,
-                pl.ds(pl.multiple_of(holder * capacity, 16), capacity),
-                pl.ds(pl.multiple_of(unit * UNIT, UNIT), UNIT),
-            ],
+            dst_ref=held.at[chunk, pl.ds(pl.multiple_of(holder * capacity, 16), capacity), :],
             send_sem=z_send.at[chunk, dw - 1],
             recv_sem=z_recv.at[chunk, dw - 1],
             device_id=wide_id(dw),
@@ -152,11 +147,10 @@
         )
 
     def z_own(chunk):
-        layer, unit = chunk // units, chunk % units
         rows = pl.ds(pl.multiple_of(wide * capacity, 16), capacity)
         return pltpu.make_async_copy(
             z_out.at[chunk, rows, :],
-            out_hbm.at[layer, rows, pl.ds(pl.multiple_of(unit * UNIT, UNIT), UNIT)],
+            held.at[chunk, rows, :],
             z_local.at[chunk],
         )
 
@@ -347,6 +341,24 @@
             z_copy(chunk, dw, wide).wait_send()
             z_copy(chunk, dw, lax.rem(wide - dw + width, width)).wait_recv()
         z_own(chunk).wait()
+
+
+def store_kernel(held, out_hbm, sem):
+    layers = out_hbm.shape[0]
+    units = held.shape[0] // layers
+    copies = [
+        pltpu.make_async_copy(
+            held.at[layer * units + unit],
+            out_hbm.at[layer, :, pl.ds(unit * UNIT, UNIT)],
+            sem.at[layer, unit],
+        )
+        for layer in range(layers)
+        for unit in range(units)
+    ]
+    for copy in copies:
+        copy.start()
+    for copy in copies:
+        copy.wait()
 
 
 def shards(
@@ -376,11 +388,11 @@
     dma = pltpu.SemaphoreType.DMA
     columns = key_value_weight.shape[2]
     ranks = adapter_down_weight.shape[2]
-    return pl.pallas_call(
+    held = pl.pallas_call(
         functools.partial(restore_kernel, sizes),
-        out_shape=jax.ShapeDtypeStruct((layers, width * capacity, block), BF16),
+        out_shape=pltpu.VMEM((chunks, width * capacity, UNIT), BF16),
         in_specs=[hbm, hbm, hbm] + [vmem] * 7,
-        out_specs=hbm,
+        out_specs=vmem,
         scratch_shapes=[
             pltpu.VMEM((layers, slots, features), BF16),
             pltpu.VMEM((layers, slots, features), BF16),
@@ -433,6 +445,15 @@
         request_length.reshape(1, slots),
         jnp.asarray(freq.reshape(half, 1)),
     )
+    return pl.pallas_call(
+        store_kernel,
+        out_shape=jax.ShapeDtypeStruct((layers, width * capacity, block), BF16),
+        in_specs=[vmem],
+        out_specs=hbm,
+        scratch_shapes=[dma((layers, units))],
+        compiler_params=pltpu.CompilerParams(vmem_limit_bytes=8 * 1024 * 1024),
+        name="store_rows",
+    )(held)
 
 
 def solution(mesh):

time: 69.3 us -> 67.5 us (0.974)
  local copies, waits for them, and re-layouts: 3.05 us -> 0 us
  Pallas kernels: 66.1 us -> 67.4 us
    unnamed x1 -> x0, local copies, waits for them, and re-layouts: 3.05 us -> none
    pallas_call x1 -> x2, Pallas kernels: 66.1 us -> 67.4 us  [the longest x1 66 us: shards(): pl.pallas_call(functools.partial(restore_kernel, sizes), out_shape=pltpu....]
where the time goes in v3:
time: 67.5 us; the launch traced here: 67.4 us
  Pallas kernels  67.4 us (100%)
    pallas_call x1, Pallas kernels, shards(): pl.pallas_call(functools.partial(restore_kernel, sizes), out_shape=pltpu....  66 us
    pallas_call x1, Pallas kernels, shards(): pl.pallas_call(store_kernel, out_shape=jax.ShapeDtypeStruct((layers, widt...  1.38 us

profile of v3, /device:TPU:0, one launch (start us, length us, event | category | flops | bytes accessed | tf_op | source)
XLA Modules:
  0.0 67.4 jit_solution(18379830223843499330)
XLA Ops:
  0.0 66.0 %restore_rows.1.held = bf16[8,1024,128]{2,1,0:T(8,128)(2,1)S(1)} custom-call(bf16[2,512,2048]{2,1,0:T(8,128)(2,1)} %hidden_hbm.1, bf16[2,2048,2048]{2,1,0:T(8,128)(2,1)} %weight_hbm.1, bf16[2,2048,128]{2,1,0:T(8,128)(2,1)} %down_hbm.1, bf16[2,128,512]{2,1,0:T(8,128)(2,1)} %up_ref.1, bf16[2,2048]{1,0:T(2,128)(2,1)} %gain_ref.1, s32[1,512]{1,0:T(1,128)} %bitcast.4, ...), custom_call_target="tpu_custom_call" | custom-call | flops 8589934592 | bytes 16777216 | tf_op jit(solution)/shard_map/restore_rows/pallas_call | solution.py:391
  66.0 1.4 %store_rows.1 = bf16[2,1024,512]{2,1,0:T(8,128)(2,1)} custom-call(bf16[8,1024,128]{2,1,0:T(8,128)(2,1)S(1)} %restore_rows.1.held), custom_call_target="tpu_custom_call" | custom-call | tf_op jit(solution)/shard_map/store_rows/pallas_call | solution.py:448

commit v4 on v3

--- a/solution.py
+++ b/solution.py
@@ -263,8 +263,12 @@
             fresh * cos_tab[kind] + pltpu.roll(fresh, HEAD_SIZE // 2, 1) * sin_tab[kind]
         ).astype(BF16)
         z_out[chunk] = jnp.dot(pick[...], rotated, preferred_element_type=F32).astype(BF16)
-        for dw in range(width - 1, 0, -1):
-            z_copy(chunk, dw, wide).start()
+        low_half = 2 * wide < width
+        for k in range(1, width):
+            down_goal = jnp.where(width - k <= wide, width - k - 1, width - k)
+            up_goal = jnp.where(k - 1 >= wide, k, k - 1)
+            goal = jnp.where(low_half, down_goal, up_goal)
+            z_copy(chunk, lax.rem(goal - wide + width, width), wide).start()
         z_own(chunk).start()
 
     hidden_copy(0).start()

time: 67.5 us -> 66.8 us (0.990)
  Pallas kernels: 67.4 us -> 66.6 us
    pallas_call x1, Pallas kernels: 66 us -> 65.2 us  [shards(): pl.pallas_call(functools.partial(restore_kernel, sizes), out_shape=pltpu....]
where the time goes in v4:
time: 66.8 us; the launch traced here: 66.6 us
  Pallas kernels  66.6 us (100%)
    pallas_call x1, Pallas kernels, shards(): pl.pallas_call(functools.partial(restore_kernel, sizes), out_shape=pltpu....  65.2 us
    pallas_call x1, Pallas kernels, shards(): pl.pallas_call(store_kernel, out_shape=jax.ShapeDtypeStruct((layers, widt...  1.38 us

profile of v4, /device:TPU:0, one launch (start us, length us, event | category | flops | bytes accessed | tf_op | source)
XLA Modules:
  0.0 66.6 jit_solution(723688574391003114)
XLA Ops:
  0.0 65.2 %restore_rows.1.held = bf16[8,1024,128]{2,1,0:T(8,128)(2,1)S(1)} custom-call(bf16[2,512,2048]{2,1,0:T(8,128)(2,1)} %hidden_hbm.1, bf16[2,2048,2048]{2,1,0:T(8,128)(2,1)} %weight_hbm.1, bf16[2,2048,128]{2,1,0:T(8,128)(2,1)} %down_hbm.1, bf16[2,128,512]{2,1,0:T(8,128)(2,1)} %up_ref.1, bf16[2,2048]{1,0:T(2,128)(2,1)} %gain_ref.1, s32[1,512]{1,0:T(1,128)} %bitcast.4, ...), custom_call_target="tpu_custom_call" | custom-call | flops 8589934592 | bytes 16777216 | tf_op jit(solution)/shard_map/restore_rows/pallas_call | solution.py:395
  65.2 1.4 %store_rows.1 = bf16[2,1024,512]{2,1,0:T(8,128)(2,1)} custom-call(bf16[8,1024,128]{2,1,0:T(8,128)(2,1)S(1)} %restore_rows.1.held), custom_call_target="tpu_custom_call" | custom-call | tf_op jit(solution)/shard_map/store_rows/pallas_call | solution.py:452
